TPU v7x, 128 devices: a whole 4x4x4 slice. The times are simulated.
128 devices in a mesh: fsdp: 64 (over z, x, y), rep: 2 (over core).
Axes of the slice: x: 4, y: 4, z: 4, core: 2. Of those that a mesh axis runs over, the one named last changes fastest.
Arguments:
- grad_parts: bfloat16 [2, 128, 1024, 1024], P('rep', None, 'fsdp'), may hold values from -6 to 6
- owner_of: int32 [128], replicated, may hold values from 0 to 127, each once
- left_stats: float32 [128, 1024, 1024], P(('fsdp', 'rep')), may hold values from -4 to 4
- right_stats: float32 [128, 1024, 1024], P(('fsdp', 'rep')), may hold values from -4 to 4
- left_root: bfloat16 [128, 1024, 1024], P(('fsdp', 'rep')), may hold values from -0.1875 to 0.1875
- right_root: bfloat16 [128, 1024, 1024], P(('fsdp', 'rep')), may hold values from -0.1875 to 0.1875
Outputs:
- new_left: float32 [128, 1024, 1024], P(('fsdp', 'rep'))
- new_right: float32 [128, 1024, 1024], P(('fsdp', 'rep'))
- direction: bfloat16 [128, 1024, 1024], P(None, ('fsdp', 'rep'))
Inputs may be any that keep to these rules, and one draw needn't show every extreme that they name: owner_of is a permutation: every owner slot holds exactly one block.
All inputs are finite; a program needn't handle non-finite values.
Results may differ from a plain program's by a relative error of at most 0.0059.
Values may be sent and summed in bfloat16 or wider, within the bound.
A program may use at most 128 MiB of HBM per device.

v0:
```python
import jax
import jax.numpy as jnp
from jax import lax
from jax.sharding import PartitionSpec as P


def body(grad_parts, owner_of, left_stats, right_stats, left_root, right_root):
    fsdp_count = lax.axis_size("fsdp")
    rep_count = lax.axis_size("rep")
    block_count = owner_of.shape[0]
    owned_count = left_stats.shape[0]
    block_size = left_stats.shape[1]
    grad_rows = grad_parts.shape[2]
    by_owner = jnp.zeros_like(owner_of).at[owner_of].set(jnp.arange(block_count, dtype=jnp.int32))
    ordered = grad_parts[0][by_owner]
    replica_total = lax.psum(ordered.astype(jnp.float32).astype(jnp.bfloat16), "rep").astype(
        jnp.float32
    )
    replica_total = replica_total.reshape(fsdp_count, rep_count, owned_count, grad_rows, block_size)
    my_rows = lax.dynamic_index_in_dim(replica_total, lax.axis_index("rep"), 1, keepdims=False)
    gradient = lax.all_to_all(
        my_rows.astype(jnp.bfloat16), "fsdp", split_axis=0, concat_axis=2, tiled=True
    ).astype(my_rows.dtype)
    gradient = gradient.reshape(owned_count, block_size, block_size)
    highest = lax.Precision.HIGHEST
    new_left = (
        left_stats + jnp.einsum("kac,kbc->kab", gradient, gradient, precision=highest) / block_size
    )
    new_right = (
        right_stats + jnp.einsum("kca,kcb->kab", gradient, gradient, precision=highest) / block_size
    )
    rounded = gradient.astype(jnp.bfloat16)
    left_applied = jnp.einsum(
        "kab,kbc->kac", left_root, rounded, preferred_element_type=jnp.float32
    ).astype(jnp.bfloat16)
    direction_owned = jnp.einsum(
        "kab,kbc->kac", left_applied, right_root, preferred_element_type=jnp.float32
    ).astype(jnp.bfloat16)
    rows_out = block_size // (fsdp_count * rep_count)
    outgoing = direction_owned.reshape(owned_count, fsdp_count * rep_count, rows_out, block_size)
    returned = lax.all_to_all(outgoing, ("fsdp", "rep"), split_axis=1, concat_axis=0, tiled=True)
    returned = returned.reshape(block_count, rows_out, block_size)
    return (new_left, new_right, returned[owner_of])


def solution(mesh):
    placed = (
        P("rep", None, "fsdp", None),
        P(),
        P(("fsdp", "rep"), None, None),
        P(("fsdp", "rep"), None, None),
        P(("fsdp", "rep"), None, None),
        P(("fsdp", "rep"), None, None),
    )
    return jax.shard_map(
        body,
        mesh=mesh,
        in_specs=placed,
        out_specs=(
            P(("fsdp", "rep"), None, None),
            P(("fsdp", "rep"), None, None),
            P(None, ("fsdp", "rep"), None),
        ),
        check_vma=False,
    )
```

profile of v0, /device:TPU:1, one launch (start us, length us, event | category | flops | bytes accessed | tf_op | source)
XLA Modules:
  0.0 148.2 jit_solution(4674225127627222761)
XLA Ops:
  7.2 0.0 copy-start
  7.2 0.0 all-reduce.2.cloned.1.call-start
  7.2 0.8 compare_select_fusion.1
  8.0 1.0 scatter_custom_fusion
  9.0 5.0 %gather_fusion = bf16[128,16,1024]{2,1,0:T(8,128)(2,1)} fusion(bf16[128,16,1024]{2,1,0:T(8,128)(2,1)} %bitcast.40, s32[1024]{0:T(1024)S(1)} %pad_clamp_fusion.1), kind=kCustom, calls=%fused_computation | custom fusion | bytes 8389120 | tf_op jit(solution)/shard_map/gather | solution.py:15
  14.1 0.0 all-reduce.2.cloned.1.call-update
  14.1 37.8 %all-reduce.2.cloned.1.call-done = bf16[64,2,1,16,1024]{4,3,1,0,2:T(8,128)(2,1)} async-done(((bf16[64,2,1,16,1024]{4,3,1,0,2:T(8,128)(2,1)}), bf16[64,2,1,16,1024]{4,3,1,0,2:T(8,128)(2,1)}) %all-reduce.2.cloned.1.call-update) | async-done | bytes 4194320 | tf_op jit(solution)/shard_map/psum | solution.py:16
  51.9 1.8 %fusion = bf16[64,1,16,1024]{3,2,1,0:T(8,128)(2,1)S(1)} fusion(bf16[64,2,1,16,1024]{4,3,1,0,2:T(8,128)(2,1)} %all-reduce.2.cloned.1.call-done, s32[]{:T(128)S(6)} %select_n.13), kind=kLoop, calls=%fused_computation.7 | loop fusion | flops 2097152 | bytes 4194308 | tf_op jit(solution)/shard_map/convert_element_type | solution.py:22
  53.7 38.5 %all_to_all.8 = bf16[64,1,16,1024]{3,2,1,0:T(8,128)(2,1)} all-to-all(bf16[64,1,16,1024]{3,2,1,0:T(8,128)(2,1)S(1)} %fusion), channel_id=1, replica_groups=mesh['fsdp'=64,'rep'=2] {'fsdp'}, dimensions={0} | all-to-all | bytes 4194304 | tf_op jit(solution)/shard_map/all_to_all | solution.py:21
  92.2 0.0 copy-done
  92.2 8.1 %convert_bitcast_fusion = bf16[1,128,8,1024]{3,2,0,1:T(8,128)(2,1)} fusion(bf16[1,1024,1024]{2,1,0:T(8,128)(2,1)S(1)} %copy-done, bf16[1024,1024]{1,0:T(8,128)(2,1)} %bitcast.41, bf16[1,1024,1024]{2,1,0:T(8,128)(2,1)} %param.10), kind=kOutput, calls=%fused_computation.14 | convolution fusion | flops 4297064448 | bytes 8388608 | tf_op jit(solution)/shard_map/kab,kbc->kac/dot_general | solution.py:36
  100.3 7.3 %all-to-all-start.1 = ((bf16[1,128,8,1024]{3,2,0,1:T(8,128)(2,1)}), bf16[1,128,8,1024]{3,2,0,1:T(8,128)(2,1)}, u32[]{:S(2)}, u32[]{:S(2)}) async-start(bf16[1,128,8,1024]{3,2,0,1:T(8,128)(2,1)} %convert_bitcast_fusion), calls=%async_computation.1 | async-start | bytes 4194304 | tf_op jit(solution)/shard_map/all_to_all | solution.py:41
  107.7 0.0 copy-start.1
  107.7 0.0 copy-start.2
  107.7 8.0 %bitcast_add_fusion.1 = f32[1,1024,1024]{2,1,0:T(8,128)} fusion(f32[1,1024,1024]{2,1,0:T(8,128)} %param.8, bf16[1024,1024]{1,0:T(8,128)(2,1)} %bitcast.42), kind=kOutput, calls=%fused_computation.5 | convolution fusion | flops 2149580800 | bytes 10485760 | tf_op jit(solution)/shard_map/kac,kbc->kab/dot_general | solution.py:27
  115.7 0.0 copy-done.1
  115.7 0.0 copy-done.2
  115.7 7.1 %bitcast_add_fusion = f32[1,1024,1024]{2,1,0:T(8,128)} fusion(f32[1,1024,1024]{2,1,0:T(8,128)S(1)} %copy-done.2, bf16[64,1,16,1024]{3,2,1,0:T(8,128)(2,1)S(1)} %copy-done.1), kind=kOutput, calls=%fused_computation.3 | convolution fusion | flops 2149580800 | bytes 10485760 | tf_op jit(solution)/shard_map/kca,kcb->kab/dot_general | solution.py:30
  122.8 15.0 %all-to-all-done.1 = bf16[1,128,8,1024]{3,2,0,1:T(8,128)(2,1)} async-done(((bf16[1,128,8,1024]{3,2,0,1:T(8,128)(2,1)}), bf16[1,128,8,1024]{3,2,0,1:T(8,128)(2,1)}, u32[]{:S(2)}, u32[]{:S(2)}) %all-to-all-start.1) | async-done | bytes 2097184 | tf_op jit(solution)/shard_map/all_to_all | solution.py:41
  137.8 3.6 %gather_fusion.1 = bf16[128,8,1024]{2,1,0:T(8,128)(2,1)} fusion(bf16[128,8,1024]{2,1,0:T(8,128)(2,1)} %bitcast.13, s32[1024]{0:T(1024)S(1)} %pad_clamp_fusion), kind=kCustom, calls=%fused_computation.1 | custom fusion | bytes 4194816 | tf_op jit(solution)/shard_map/gather | solution.py:43
  (4 shorter events, 0.0 us)
Async XLA Ops:
  7.2 85.0 %copy-start = (bf16[1,1024,1024]{2,1,0:T(8,128)(2,1)S(1)}, bf16[1,1024,1024]{2,1,0:T(8,128)(2,1)}, u32[]{:S(2)}) copy-start(bf16[1,1024,1024]{2,1,0:T(8,128)(2,1)} %param.11) | copy-start | bytes 6291460
  7.2 44.7 %all-reduce.2.cloned.1.call-start = ((), (), s32[]{:S(2)}) async-start(), calls=%async_computation.2 | async-start | bytes 8388608 | tf_op jit(solution)/shard_map/psum | solution.py:16
  100.3 37.5 %all-to-all-start.1 = ((bf16[1,128,8,1024]{3,2,0,1:T(8,128)(2,1)}), bf16[1,128,8,1024]{3,2,0,1:T(8,128)(2,1)}, u32[]{:S(2)}, u32[]{:S(2)}) async-start(bf16[1,128,8,1024]{3,2,0,1:T(8,128)(2,1)} %convert_bitcast_fusion), calls=%async_computation.1 | async-start | bytes 4194304 | tf_op jit(solution)/shard_map/all_to_all | solution.py:41
  107.7 8.0 %copy-start.1 = (bf16[64,1,16,1024]{3,2,1,0:T(8,128)(2,1)S(1)}, bf16[64,1,16,1024]{3,2,1,0:T(8,128)(2,1)}, u32[]{:S(2)}) copy-start(bf16[64,1,16,1024]{3,2,1,0:T(8,128)(2,1)} %all_to_all.8) | copy-start | bytes 6291460
  107.7 8.0 %copy-start.2 = (f32[1,1024,1024]{2,1,0:T(8,128)S(1)}, f32[1,1024,1024]{2,1,0:T(8,128)}, u32[]{:S(2)}) copy-start(f32[1,1024,1024]{2,1,0:T(8,128)} %param.9) | copy-start | bytes 12582916
Sparse Core Ops, SparseCore 0:
  14.2 37.6 all-reduce.1
where the time goes:
time: 149 us; the launch traced here: 148 us
  waiting for transfers between devices  52.8 us (35%)
  blocking collectives  38.5 us (26%)
  matrix products  23.3 us (16%)
  between operations  14.1 us (9%)
  local copies, waits for them, and re-layouts  9.6 us (6%)
  starting transfers between devices  7.37 us (5%)
  other arithmetic  2.58 us (2%)
    all_to_all x1, blocking collectives, body(): lax.all_to_all(my_rows.astype(jnp.bfloat16), 'fsdp', split_axis=0, concat...  38.5 us
    psum x1, waiting for transfers between devices, body(): lax.psum(ordered.astype(jnp.float32).astype(jnp.bfloat16), 'rep')  37.8 us
    all_to_all x1, waiting for transfers between devices, body(): lax.all_to_all(outgoing, ('fsdp', 'rep'), split_axis=1, concat_axis=0, ti...  15 us
    dot_general x1, matrix products, body(): jnp.einsum('kab,kbc->kac', left_applied, right_root, preferred_element_ty...  8.12 us
    dot_general x1, matrix products, body(): jnp.einsum('kac,kbc->kab', gradient, gradient, precision=highest)  7.99 us
    all_to_all x1, starting transfers between devices, body(): lax.all_to_all(outgoing, ('fsdp', 'rep'), split_axis=1, concat_axis=0, ti...  7.33 us
    dot_general x1, matrix products, body(): jnp.einsum('kca,kcb->kab', gradient, gradient, precision=highest)  7.14 us
    gather x1, local copies, waits for them, and re-layouts, body(): ordered = grad_parts[0][by_owner]  5.02 us
  transfers between devices with their start and end apart: 2, of which 2 were waited for; matrix products, arithmetic and copies ran while one was open for 10% of the time, Pallas kernels for 0%

commit v1 on v0

v1 whole, which is shorter than its diff:
```python
import jax
import jax.numpy as jnp
from jax import lax
from jax.experimental import pallas as pl
from jax.experimental.pallas import tpu as pltpu
from jax.sharding import PartitionSpec as P

MESH = pl.DeviceIdType.MESH
CHIPS = 64
BS = 1024
BLOCKS = 128
ROWS = BS // CHIPS
HALF = ROWS // 2
CHUNK = 8
LEAP = 21
BF16 = jnp.bfloat16
F32 = jnp.float32


def partner_chip(me, step):
    o = lax.rem(step * LEAP, CHIPS)
    z = lax.rem(lax.div(me, 16) + lax.div(o, 16), 4)
    x = lax.rem(lax.div(me, 4) + lax.div(o, 4), 4)
    y = lax.rem(me + o, 4)
    return z * 16 + x * 4 + y


def kernel(
    by_owner, owner_of, grad_hbm, lstat_hbm, rstat_hbm, lroot_hbm, rroot_hbm,
    new_left, new_right, direction,
    grad, stage, partner_part, summed, gathered, lroot, lperm, rroot, outgoing, returned,
    load_sem, swap_send, swap_recv, fwd_send, fwd_recv, back_send, back_recv,
):
    f = lax.axis_index("fsdp")
    r = lax.axis_index("rep")
    other = 1 - r
    me = 2 * f + r

    load_grad = pltpu.make_async_copy(grad_hbm.at[0], grad, load_sem.at[0])
    load_grad.start()

    barrier = pltpu.get_barrier_semaphore()

    @pl.loop(1, 2 * CHIPS)
    def _(k):
        d = lax.rem(me + k, 2 * CHIPS)
        pl.semaphore_signal(
            barrier, inc=1, device_id=(lax.div(d, 2), lax.rem(d, 2)), device_id_type=MESH
        )

    loads = [
        pltpu.make_async_copy(lroot_hbm.at[0], lroot, load_sem.at[1]),
        pltpu.make_async_copy(rroot_hbm.at[0], rroot, load_sem.at[2]),
        pltpu.make_async_copy(lstat_hbm.at[0], new_left.at[0], load_sem.at[3]),
        pltpu.make_async_copy(rstat_hbm.at[0], new_right.at[0], load_sem.at[4]),
    ]
    for load in loads:
        load.start()
    load_grad.wait()
    pl.semaphore_wait(barrier, 2 * CHIPS - 1)

    def swap(c):
        part = pl.ds(c * CHUNK, CHUNK)
        return pltpu.make_async_remote_copy(
            stage.at[part], partner_part.at[part], swap_send.at[c], swap_recv.at[c],
            device_id=(f, other), device_id_type=MESH,
        )

    @pl.loop(0, CHIPS // CHUNK)
    def _(c):
        @pl.loop(0, CHUNK)
        def _(j):
            i = c * CHUNK + j
            stage[i] = grad[by_owner[2 * partner_chip(f, i) + other]]

        swap(c).start()

    @pl.loop(0, CHIPS // CHUNK)
    def _(c):
        swap(c).wait_recv()

        @pl.loop(0, CHUNK)
        def _(j):
            i = c * CHUNK + j
            to = partner_chip(f, i)
            mine = grad[by_owner[2 * to + r]].astype(F32)
            summed[i] = (mine + partner_part[i].astype(F32)).astype(BF16)

            @pl.when(i > 0)
            def _():
                pltpu.make_async_remote_copy(
                    summed.at[i], gathered.at[f], fwd_send, fwd_recv,
                    device_id=(to, r), device_id_type=MESH,
                ).start()

    gathered[f] = summed[0]
    for load in loads:
        load.wait()

    @pl.loop(0, CHIPS)
    def _(i):
        lperm[i] = lroot[pl.ds(pl.multiple_of(partner_chip(f, i) * ROWS, ROWS), ROWS), :]

    rest = pl.ds(0, CHIPS - 1)
    pltpu.make_async_copy(gathered.at[rest], gathered.at[rest], fwd_recv).wait()

    @pl.loop(0, CHIPS // CHUNK)
    def _(c):
        part = lperm[pl.ds(c * CHUNK, CHUNK)].reshape(CHUNK * ROWS, BS)
        whole = gathered[...].reshape(BS, BS)
        applied = jnp.dot(part, whole, preferred_element_type=F32).astype(BF16)
        done = jnp.dot(applied, rroot[...], preferred_element_type=F32)
        outgoing[pl.ds(c * 2 * CHUNK, 2 * CHUNK)] = done.reshape(2 * CHUNK, HALF, BS).astype(BF16)

        @pl.loop(0, 2 * CHUNK)
        def _(j):
            h = c * 2 * CHUNK + j
            to = partner_chip(f, lax.div(h, 2))
            core = lax.rem(h, 2)

            @pl.when(2 * to + core != me)
            def _():
                pltpu.make_async_remote_copy(
                    outgoing.at[h], returned.at[me], back_send, back_recv,
                    device_id=(to, core), device_id_type=MESH,
                ).start()

    returned[me] = outgoing[r]

    @pl.loop(0, 4)
    def _(c):
        rows = pl.ds(pl.multiple_of(c * 256, 256), 256)
        whole = gathered[...].reshape(BS, BS)
        part = gathered[pl.ds(c * 16, 16)].reshape(256, BS)
        gram = lax.dot_general(part, whole, (((1,), (1,)), ((), ())), preferred_element_type=F32)
        new_left[0, rows, :] += gram * (1.0 / BS)

    @pl.loop(0, 4)
    def _(c):
        rows = pl.ds(pl.multiple_of(c * 256, 256), 256)
        whole = gathered[...].reshape(BS, BS)
        part = gathered[:, :, rows].reshape(BS, 256)
        gram = lax.dot_general(part, whole, (((0,), (0,)), ((), ())), preferred_element_type=F32)
        new_right[0, rows, :] += gram * (1.0 / BS)

    @pl.loop(0, CHIPS // CHUNK)
    def _(c):
        swap(c).wait_send()

    pltpu.make_async_copy(gathered.at[rest], gathered.at[rest], fwd_send).wait()
    all_but_me = pl.ds(0, BLOCKS - 1)
    pltpu.make_async_copy(returned.at[all_but_me], returned.at[all_but_me], back_send).wait()
    pltpu.make_async_copy(returned.at[all_but_me], returned.at[all_but_me], back_recv).wait()

    @pl.loop(0, BLOCKS)
    def _(b):
        direction[b] = returned[owner_of[b]]


def body(grad_parts, owner_of, left_stats, right_stats, left_root, right_root):
    blocks = jnp.arange(BLOCKS, dtype=jnp.int32)
    by_owner = jnp.sum(
        jnp.where(owner_of[None, :] == blocks[:, None], blocks[None, :], 0), axis=1, dtype=jnp.int32
    )
    smem = pl.BlockSpec(memory_space=pltpu.SMEM)
    anywhere = pl.BlockSpec(memory_space=pl.ANY)
    vmem = pl.BlockSpec(memory_space=pltpu.VMEM)
    return pl.pallas_call(
        kernel,
        out_shape=(
            jax.ShapeDtypeStruct((1, BS, BS), F32),
            jax.ShapeDtypeStruct((1, BS, BS), F32),
            jax.ShapeDtypeStruct((BLOCKS, HALF, BS), BF16),
        ),
        in_specs=[smem, smem] + [anywhere] * 5,
        out_specs=(vmem, vmem, vmem),
        scratch_shapes=[
            pltpu.VMEM((BLOCKS, ROWS, BS), BF16),
            pltpu.VMEM((CHIPS, ROWS, BS), BF16),
            pltpu.VMEM((CHIPS, ROWS, BS), BF16),
            pltpu.VMEM((CHIPS, ROWS, BS), BF16),
            pltpu.VMEM((CHIPS, ROWS, BS), BF16),
            pltpu.VMEM((BS, BS), BF16),
            pltpu.VMEM((CHIPS, ROWS, BS), BF16),
            pltpu.VMEM((BS, BS), BF16),
            pltpu.VMEM((BLOCKS, HALF, BS), BF16),
            pltpu.VMEM((BLOCKS, HALF, BS), BF16),
            pltpu.SemaphoreType.DMA((5,)),
            pltpu.SemaphoreType.DMA((CHIPS // CHUNK,)),
            pltpu.SemaphoreType.DMA((CHIPS // CHUNK,)),
            pltpu.SemaphoreType.DMA,
            pltpu.SemaphoreType.DMA,
            pltpu.SemaphoreType.DMA,
            pltpu.SemaphoreType.DMA,
        ],
        compiler_params=pltpu.CompilerParams(
            collective_id=0, has_side_effects=True, vmem_limit_bytes=56 * 2**20
        ),
        cost_estimate=pl.CostEstimate(
            flops=8 * BS**3, bytes_accessed=26 * 2**20, transcendentals=0
        ),
        name="shampoo_step",
    )(by_owner, owner_of, grad_parts, left_stats, right_stats, left_root, right_root)


def solution(mesh):
    placed = (
        P("rep", None, "fsdp", None),
        P(),
        P(("fsdp", "rep"), None, None),
        P(("fsdp", "rep"), None, None),
        P(("fsdp", "rep"), None, None),
        P(("fsdp", "rep"), None, None),
    )
    return jax.shard_map(
        body,
        mesh=mesh,
        in_specs=placed,
        out_specs=(
            P(("fsdp", "rep"), None, None),
            P(("fsdp", "rep"), None, None),
            P(None, ("fsdp", "rep"), None),
        ),
        check_vma=False,
    )
```

time: 149 us -> 85.8 us (0.58)
  Pallas kernels: 0 us -> 74.3 us
  waiting for transfers between devices: 52.8 us -> 0 us
  blocking collectives: 38.5 us -> 0 us
  matrix products: 23.3 us -> 0 us
  between operations: 14.1 us -> 0.65 us
  starting transfers between devices: 7.37 us -> 0 us
    pallas_call x0 -> x1, Pallas kernels: none -> 74.3 us  [body(): pl.pallas_call(kernel, out_shape=(jax.ShapeDtypeStruct((1, BS, BS), F32),...]
    all_to_all x1 -> x0, blocking collectives: 38.5 us -> none  [body(): lax.all_to_all(my_rows.astype(jnp.bfloat16), 'fsdp', split_axis=0, concat...]
    psum x1 -> x0, waiting for transfers between devices: 37.8 us -> none  [body(): lax.psum(ordered.astype(jnp.float32).astype(jnp.bfloat16), 'rep')]
    dot_general x3 -> x0, matrix products: 23.3 us -> none  [the longest x1 8.12 us: body(): jnp.einsum('kab,kbc->kac', left_applied, right_root, preferred_element_ty...]
    all_to_all x1 -> x0, waiting for transfers between devices: 15 us -> none  [body(): lax.all_to_all(outgoing, ('fsdp', 'rep'), split_axis=1, concat_axis=0, ti...]
    unnamed x6 -> x7, local copies, waits for them, and re-layouts: 0.02 us -> 9.37 us
    gather x2 -> x0, local copies, waits for them, and re-layouts: 8.61 us -> none  [the longest x1 5.02 us: body(): ordered = grad_parts[0][by_owner]]
    all_to_all x1 -> x0, starting transfers between devices: 7.33 us -> none  [body(): lax.all_to_all(outgoing, ('fsdp', 'rep'), split_axis=1, concat_axis=0, ti...]
  transfers between devices with their start and end apart: 2 -> 0, of which waited for: 2 -> 0; matrix products, arithmetic and copies ran while one was open for 10% -> 0% of each run, Pallas kernels for 0% -> 0%
where the time goes in v1:
time: 85.8 us; the launch traced here: 85.6 us
  Pallas kernels  74.3 us (87%)
  local copies, waits for them, and re-layouts  9.37 us (11%)
  other arithmetic  1.28 us (1%)
    pallas_call x1, Pallas kernels, body(): pl.pallas_call(kernel, out_shape=(jax.ShapeDtypeStruct((1, BS, BS), F32),...  74.3 us
    unnamed x7, local copies, waits for them, and re-layouts  9.37 us

profile of v1, /device:TPU:1, one launch (start us, length us, event | category | flops | bytes accessed | tf_op | source)
XLA Modules:
  0.0 85.6 jit_solution(8012878434554751591)
XLA Ops:
  0.6 1.3 %select_reduce_fusion.by_owner = s32[128]{0:T(128)} fusion(s32[128]{0:T(128)} %owner_of.1), kind=kLoop, calls=%fused_computation | loop fusion | flops 49024 | bytes 1024 | tf_op jit(solution)/shard_map/reduce_sum | solution.py:162
  1.9 74.3 %shampoo_step.1 = (f32[1,1024,1024]{2,1,0:T(8,128)}, f32[1,1024,1024]{2,1,0:T(8,128)}, bf16[128,8,1024]{2,1,0:T(8,128)(2,1)}) custom-call(s32[128]{0:T(128)} %select_reduce_fusion.by_owner, s32[128]{0:T(128)} %owner_of.1, bf16[1,128,16,1024]{3,2,1,0:T(8,128)(2,1)} %grad_hbm.1, f32[1,1024,1024]{2,1,0:T(8,128)} %lstat_hbm.1, f32[1,1024,1024]{2,1,0:T(8,128)} %rstat_hbm.1, ...), custom_call_target="tpu_custom_call" | custom-call | flops 8589934592 | bytes 27262976 | tf_op jit(solution)/shard_map/shampoo_step/pallas_call | solution.py:168
  76.2 0.0 copy-start
  76.2 4.9 %copy.12 = f32[1,1024,1024]{2,1,0:T(8,128)} copy(f32[1,1024,1024]{2,1,0:T(8,128)} %get-tuple-element.6) | data formatting | bytes 8388608
  81.2 0.0 copy-done
  81.2 0.0 copy-start.1
  81.2 2.1 %copy.13 = f32[1,1024,1024]{2,1,0:T(8,128)} copy(f32[1,1024,1024]{2,1,0:T(8,128)S(1)} %copy-done) | data formatting | bytes 8388608
  83.3 1.0 %copy-done.1 = bf16[128,8,1024]{2,1,0:T(8,128)(2,1)S(1)} copy-done((bf16[128,8,1024]{2,1,0:T(8,128)(2,1)S(1)}, bf16[128,8,1024]{2,1,0:T(8,128)(2,1)}, u32[]{:S(2)}) %copy-start.1) | copy-done | bytes 2097176
  84.3 1.3 %copy.14 = bf16[128,8,1024]{2,1,0:T(8,128)(2,1)} copy(bf16[128,8,1024]{2,1,0:T(8,128)(2,1)S(1)} %copy-done.1) | data formatting | bytes 4194304
Async XLA Ops:
  76.2 5.0 %copy-start = (f32[1,1024,1024]{2,1,0:T(8,128)S(1)}, f32[1,1024,1024]{2,1,0:T(8,128)}, u32[]{:S(2)}) copy-start(f32[1,1024,1024]{2,1,0:T(8,128)} %get-tuple-element.7) | copy-start | bytes 12582916
  81.2 3.1 %copy-start.1 = (bf16[128,8,1024]{2,1,0:T(8,128)(2,1)S(1)}, bf16[128,8,1024]{2,1,0:T(8,128)(2,1)}, u32[]{:S(2)}) copy-start(bf16[128,8,1024]{2,1,0:T(8,128)(2,1)} %get-tuple-element.8) | copy-start | bytes 6291460

commit v2 on v1

--- a/solution.py
+++ b/solution.py
@@ -12,7 +12,7 @@
 ROWS = BS // CHIPS
 HALF = ROWS // 2
 CHUNK = 8
-LEAP = 21
+LEAP = 27
 BF16 = jnp.bfloat16
 F32 = jnp.float32
 
@@ -26,9 +26,10 @@
 
 
 def kernel(
-    by_owner, owner_of, grad_hbm, lstat_hbm, rstat_hbm, lroot_hbm, rroot_hbm,
-    new_left, new_right, direction,
-    grad, stage, partner_part, summed, gathered, lroot, lperm, rroot, outgoing, returned,
+    owner_of, grad_hbm, lstat_hbm, rstat_hbm, lroot_hbm, rroot_hbm,
+    new_left, new_right, returned,
+    grad, stage, partner_part, summed, gathered, lroot, lperm, rroot, outgoing,
+    by_owner_v, by_owner,
     load_sem, swap_send, swap_recv, fwd_send, fwd_recv, back_send, back_recv,
 ):
     f = lax.axis_index("fsdp")
@@ -56,6 +57,13 @@
     ]
     for load in loads:
         load.start()
+    slot = lax.broadcasted_iota(jnp.int32, (BLOCKS, BLOCKS), 0)
+    block = lax.broadcasted_iota(jnp.int32, (BLOCKS, BLOCKS), 1)
+    held = jnp.where(jnp.broadcast_to(owner_of[...], (BLOCKS, BLOCKS)) == slot, block, 0)
+    by_owner_v[...] = jnp.max(held.T, axis=0, keepdims=True)
+    to_smem = pltpu.make_async_copy(by_owner_v, by_owner, load_sem.at[5])
+    to_smem.start()
+    to_smem.wait()
     load_grad.wait()
     pl.semaphore_wait(barrier, 2 * CHIPS - 1)
 
@@ -71,7 +79,7 @@
         @pl.loop(0, CHUNK)
         def _(j):
             i = c * CHUNK + j
-            stage[i] = grad[by_owner[2 * partner_chip(f, i) + other]]
+            stage[i] = grad[by_owner[0, 2 * partner_chip(f, i) + other]]
 
         swap(c).start()
 
@@ -83,7 +91,7 @@
         def _(j):
             i = c * CHUNK + j
             to = partner_chip(f, i)
-            mine = grad[by_owner[2 * to + r]].astype(F32)
+            mine = grad[by_owner[0, 2 * to + r]].astype(F32)
             summed[i] = (mine + partner_part[i].astype(F32)).astype(BF16)
 
             @pl.when(i > 0)
@@ -152,55 +160,78 @@
     pltpu.make_async_copy(returned.at[all_but_me], returned.at[all_but_me], back_send).wait()
     pltpu.make_async_copy(returned.at[all_but_me], returned.at[all_but_me], back_recv).wait()
 
+
+def write_out(owner_of, left, right, returned, new_left, new_right, direction, sem):
+    writes = [
+        pltpu.make_async_copy(left, new_left, sem.at[0]),
+        pltpu.make_async_copy(right, new_right, sem.at[1]),
+    ]
+    for write in writes:
+        write.start()
+
     @pl.loop(0, BLOCKS)
     def _(b):
-        direction[b] = returned[owner_of[b]]
+        pltpu.make_async_copy(returned.at[owner_of[b]], direction.at[b], sem.at[2]).start()
+
+    for write in writes:
+        write.wait()
+    pltpu.make_async_copy(returned, direction, sem.at[2]).wait()
 
 
 def body(grad_parts, owner_of, left_stats, right_stats, left_root, right_root):
-    blocks = jnp.arange(BLOCKS, dtype=jnp.int32)
-    by_owner = jnp.sum(
-        jnp.where(owner_of[None, :] == blocks[:, None], blocks[None, :], 0), axis=1, dtype=jnp.int32
-    )
-    smem = pl.BlockSpec(memory_space=pltpu.SMEM)
     anywhere = pl.BlockSpec(memory_space=pl.ANY)
     vmem = pl.BlockSpec(memory_space=pltpu.VMEM)
+    smem = pl.BlockSpec(memory_space=pltpu.SMEM)
+    left, right, returned = pl.pallas_call(
+        kernel,
+        out_shape=(
+            pltpu.VMEM((1, BS, BS), F32),
+            pltpu.VMEM((1, BS, BS), F32),
+            pltpu.VMEM((BLOCKS, HALF, BS), BF16),
+        ),
+        in_specs=[vmem] + [anywhere] * 5,
+        out_specs=(vmem, vmem, vmem),
+        scratch_shapes=[
+            pltpu.VMEM((BLOCKS, ROWS, BS), BF16),
+            pltpu.VMEM((CHIPS, ROWS, BS), BF16),
+            pltpu.VMEM((CHIPS, ROWS, BS), BF16),
+            pltpu.VMEM((CHIPS, ROWS, BS), BF16),
+            pltpu.VMEM((CHIPS, ROWS, BS), BF16),
+            pltpu.VMEM((BS, BS), BF16),
+            pltpu.VMEM((CHIPS, ROWS, BS), BF16),
+            pltpu.VMEM((BS, BS), BF16),
+            pltpu.VMEM((BLOCKS, HALF, BS), BF16),
+            pltpu.VMEM((1, BLOCKS), jnp.int32),
+            pltpu.SMEM((1, BLOCKS), jnp.int32),
+            pltpu.SemaphoreType.DMA((6,)),
+            pltpu.SemaphoreType.DMA((CHIPS // CHUNK,)),
+            pltpu.SemaphoreType.DMA((CHIPS // CHUNK,)),
+            pltpu.SemaphoreType.DMA,
+            pltpu.SemaphoreType.DMA,
+            pltpu.SemaphoreType.DMA,
+            pltpu.SemaphoreType.DMA,
+        ],
+        compiler_params=pltpu.CompilerParams(
+            collective_id=0, has_side_effects=True, vmem_limit_bytes=52 * 2**20
+        ),
+        cost_estimate=pl.CostEstimate(
+            flops=8 * BS**3, bytes_accessed=16 * 2**20, transcendentals=0
+        ),
+        name="shampoo_step",
+    )(owner_of[None], grad_parts, left_stats, right_stats, left_root, right_root)
     return pl.pallas_call(
-        kernel,
+        write_out,
         out_shape=(
             jax.ShapeDtypeStruct((1, BS, BS), F32),
             jax.ShapeDtypeStruct((1, BS, BS), F32),
             jax.ShapeDtypeStruct((BLOCKS, HALF, BS), BF16),
         ),
-        in_specs=[smem, smem] + [anywhere] * 5,
-        out_specs=(vmem, vmem, vmem),
-        scratch_shapes=[
-            pltpu.VMEM((BLOCKS, ROWS, BS), BF16),
-            pltpu.VMEM((CHIPS, ROWS, BS), BF16),
-            pltpu.VMEM((CHIPS, ROWS, BS), BF16),
-            pltpu.VMEM((CHIPS, ROWS, BS), BF16),
-            pltpu.VMEM((CHIPS, ROWS, BS), BF16),
-            pltpu.VMEM((BS, BS), BF16),
-            pltpu.VMEM((CHIPS, ROWS, BS), BF16),
-            pltpu.VMEM((BS, BS), BF16),
-            pltpu.VMEM((BLOCKS, HALF, BS), BF16),
-            pltpu.VMEM((BLOCKS, HALF, BS), BF16),
-            pltpu.SemaphoreType.DMA((5,)),
-            pltpu.SemaphoreType.DMA((CHIPS // CHUNK,)),
-            pltpu.SemaphoreType.DMA((CHIPS // CHUNK,)),
-            pltpu.SemaphoreType.DMA,
-            pltpu.SemaphoreType.DMA,
-            pltpu.SemaphoreType.DMA,
-            pltpu.SemaphoreType.DMA,
-        ],
-        compiler_params=pltpu.CompilerParams(
-            collective_id=0, has_side_effects=True, vmem_limit_bytes=56 * 2**20
-        ),
-        cost_estimate=pl.CostEstimate(
-            flops=8 * BS**3, bytes_accessed=26 * 2**20, transcendentals=0
-        ),
-        name="shampoo_step",
-    )(by_owner, owner_of, grad_parts, left_stats, right_stats, left_root, right_root)
+        in_specs=[smem] + [anywhere] * 3,
+        out_specs=(anywhere, anywhere, anywhere),
+        scratch_shapes=[pltpu.SemaphoreType.DMA((3,))],
+        compiler_params=pltpu.CompilerParams(vmem_limit_bytes=2 * 2**20),
+        name="write_out",
+    )(owner_of, left, right, returned)
 
 
 def solution(mesh):

time: 85.8 us -> 72.6 us (0.85)
  local copies, waits for them, and re-layouts: 9.37 us -> 0.01 us
  Pallas kernels: 74.3 us -> 71.8 us
  other arithmetic: 1.28 us -> 0 us
    unnamed x7 -> x2, local copies, waits for them, and re-layouts: 9.37 us -> 0.01 us
    pallas_call x1 -> x2, Pallas kernels: 74.3 us -> 71.8 us  [the longest x1 67.4 us: body(): pl.pallas_call(kernel, out_shape=(pltpu.VMEM((1, BS, BS), F32), pltpu.VME...]
    reduce_sum x1 -> x0, other arithmetic: 1.28 us -> none  [body(): jnp.sum(jnp.where(owner_of[None, :] == blocks[:, None], blocks[None, :],...]
where the time goes in v2:
time: 72.6 us; the launch traced here: 72.5 us
  Pallas kernels  71.8 us (99%)
    pallas_call x1, Pallas kernels, body(): pl.pallas_call(kernel, out_shape=(pltpu.VMEM((1, BS, BS), F32), pltpu.VME...  67.4 us
    pallas_call x1, Pallas kernels, body(): pl.pallas_call(write_out, out_shape=(jax.ShapeDtypeStruct((1, BS, BS), F3...  4.42 us

profile of v2, /device:TPU:1, one launch (start us, length us, event | category | flops | bytes accessed | tf_op | source)
XLA Modules:
  0.0 72.5 jit_solution(3266493526362511814)
XLA Ops:
  0.6 0.0 copy-start
  0.6 67.4 %shampoo_step.1 = (f32[1,1024,1024]{2,1,0:T(8,128)S(1)}, f32[1,1024,1024]{2,1,0:T(8,128)S(1)}, bf16[128,8,1024]{2,1,0:T(8,128)(2,1)S(1)}) custom-call(s32[1,128]{1,0:T(1,128)} %bitcast.1, bf16[1,128,16,1024]{3,2,1,0:T(8,128)(2,1)} %grad_hbm.1, f32[1,1024,1024]{2,1,0:T(8,128)} %lstat_hbm.1, f32[1,1024,1024]{2,1,0:T(8,128)} %rstat_hbm.1, ...), custom_call_target="tpu_custom_call" | custom-call | flops 8589934592 | bytes 16777216 | tf_op jit(solution)/shard_map/shampoo_step/pallas_call | solution.py:185
  68.1 0.0 copy-done
  68.1 4.4 %write_out.1 = (f32[1,1024,1024]{2,1,0:T(8,128)}, f32[1,1024,1024]{2,1,0:T(8,128)}, bf16[128,8,1024]{2,1,0:T(8,128)(2,1)}) custom-call(s32[128]{0:T(128)S(1)} %copy-done, f32[1,1024,1024]{2,1,0:T(8,128)S(1)} %get-tuple-element.6.left, f32[1,1024,1024]{2,1,0:T(8,128)S(1)} %get-tuple-element.7.right, bf16[128,8,1024]{2,1,0:T(8,128)(2,1)S(1)} %get-tuple-element.8.returned), custom_call_target="tpu_custom_call" | custom-call | tf_op jit(solution)/shard_map/write_out/pallas_call | solution.py:222
Async XLA Ops:
  0.6 67.4 %copy-start = (s32[128]{0:T(128)S(1)}, s32[128]{0:T(128)}, u32[]{:S(2)}) copy-start(s32[128]{0:T(128)} %owner_of.1) | copy-start | bytes 1540

commit v3 on v2

--- a/solution.py
+++ b/solution.py
@@ -30,7 +30,7 @@
     new_left, new_right, returned,
     grad, stage, partner_part, summed, gathered, lroot, lperm, rroot, outgoing,
     by_owner_v, by_owner,
-    load_sem, swap_send, swap_recv, fwd_send, fwd_recv, back_send, back_recv,
+    load_sem, swap_send, swap_recv, fwd_send, fwd_recv, back_send, back_recv, go,
 ):
     f = lax.axis_index("fsdp")
     r = lax.axis_index("rep")
@@ -42,11 +42,12 @@
 
     barrier = pltpu.get_barrier_semaphore()
 
-    @pl.loop(1, 2 * CHIPS)
+    pl.semaphore_signal(barrier, inc=1, device_id=(f, other), device_id_type=MESH)
+
+    @pl.loop(1, CHIPS)
     def _(k):
-        d = lax.rem(me + k, 2 * CHIPS)
         pl.semaphore_signal(
-            barrier, inc=1, device_id=(lax.div(d, 2), lax.rem(d, 2)), device_id_type=MESH
+            barrier, inc=1, device_id=(lax.rem(f + k, CHIPS), r), device_id_type=MESH
         )
 
     loads = [
@@ -55,8 +56,6 @@
         pltpu.make_async_copy(lstat_hbm.at[0], new_left.at[0], load_sem.at[3]),
         pltpu.make_async_copy(rstat_hbm.at[0], new_right.at[0], load_sem.at[4]),
     ]
-    for load in loads:
-        load.start()
     slot = lax.broadcasted_iota(jnp.int32, (BLOCKS, BLOCKS), 0)
     block = lax.broadcasted_iota(jnp.int32, (BLOCKS, BLOCKS), 1)
     held = jnp.where(jnp.broadcast_to(owner_of[...], (BLOCKS, BLOCKS)) == slot, block, 0)
@@ -65,7 +64,9 @@
     to_smem.start()
     to_smem.wait()
     load_grad.wait()
-    pl.semaphore_wait(barrier, 2 * CHIPS - 1)
+    for load in loads:
+        load.start()
+    pl.semaphore_wait(barrier, CHIPS)
 
     def swap(c):
         part = pl.ds(c * CHUNK, CHUNK)
@@ -83,6 +84,12 @@
 
         swap(c).start()
 
+    def forward(i, to):
+        return pltpu.make_async_remote_copy(
+            summed.at[i], gathered.at[f], fwd_send.at[lax.div(i, 32)], fwd_recv,
+            device_id=(to, r), device_id_type=MESH,
+        )
+
     @pl.loop(0, CHIPS // CHUNK)
     def _(c):
         swap(c).wait_recv()
@@ -94,12 +101,9 @@
             mine = grad[by_owner[0, 2 * to + r]].astype(F32)
             summed[i] = (mine + partner_part[i].astype(F32)).astype(BF16)
 
-            @pl.when(i > 0)
+            @pl.when(jnp.logical_and(i > 0, r == 0))
             def _():
-                pltpu.make_async_remote_copy(
-                    summed.at[i], gathered.at[f], fwd_send, fwd_recv,
-                    device_id=(to, r), device_id_type=MESH,
-                ).start()
+                forward(i, to).start()
 
     gathered[f] = summed[0]
     for load in loads:
@@ -110,6 +114,21 @@
         lperm[i] = lroot[pl.ds(pl.multiple_of(partner_chip(f, i) * ROWS, ROWS), ROWS), :]
 
     rest = pl.ds(0, CHIPS - 1)
+
+    @pl.when(r == 0)
+    def _():
+        soon = pl.ds(0, 32 - 1)
+        pltpu.make_async_copy(gathered.at[soon], gathered.at[soon], fwd_send.at[0]).wait()
+        pl.semaphore_signal(go, inc=1, device_id=(f, other), device_id_type=MESH)
+
+    @pl.when(r == 1)
+    def _():
+        pl.semaphore_wait(go, 1)
+
+        @pl.loop(1, CHIPS)
+        def _(i):
+            forward(i, partner_chip(f, i)).start()
+
     pltpu.make_async_copy(gathered.at[rest], gathered.at[rest], fwd_recv).wait()
 
     @pl.loop(0, CHIPS // CHUNK)
@@ -155,7 +174,14 @@
     def _(c):
         swap(c).wait_send()
 
-    pltpu.make_async_copy(gathered.at[rest], gathered.at[rest], fwd_send).wait()
+    late = pl.ds(0, 32)
+    pltpu.make_async_copy(gathered.at[late], gathered.at[late], fwd_send.at[1]).wait()
+
+    @pl.when(r == 1)
+    def _():
+        soon = pl.ds(0, 32 - 1)
+        pltpu.make_async_copy(gathered.at[soon], gathered.at[soon], fwd_send.at[0]).wait()
+
     all_but_me = pl.ds(0, BLOCKS - 1)
     pltpu.make_async_copy(returned.at[all_but_me], returned.at[all_but_me], back_send).wait()
     pltpu.make_async_copy(returned.at[all_but_me], returned.at[all_but_me], back_recv).wait()
@@ -206,10 +232,11 @@
             pltpu.SemaphoreType.DMA((6,)),
             pltpu.SemaphoreType.DMA((CHIPS // CHUNK,)),
             pltpu.SemaphoreType.DMA((CHIPS // CHUNK,)),
+            pltpu.SemaphoreType.DMA((2,)),
             pltpu.SemaphoreType.DMA,
             pltpu.SemaphoreType.DMA,
             pltpu.SemaphoreType.DMA,
-            pltpu.SemaphoreType.DMA,
+            pltpu.SemaphoreType.REGULAR,
         ],
         compiler_params=pltpu.CompilerParams(
             collective_id=0, has_side_effects=True, vmem_limit_bytes=52 * 2**20

time: 72.6 us -> 67.6 us (0.931)
  Pallas kernels: 71.8 us -> 66.7 us
    pallas_call x1, Pallas kernels: 67.4 us -> 62.3 us  [body(): pl.pallas_call(kernel, out_shape=(pltpu.VMEM((1, BS, BS), F32), pltpu.VME...]
where the time goes in v3:
time: 67.6 us; the launch traced here: 67.4 us
  Pallas kernels  66.7 us (99%)
    pallas_call x1, Pallas kernels, body(): pl.pallas_call(kernel, out_shape=(pltpu.VMEM((1, BS, BS), F32), pltpu.VME...  62.3 us
    pallas_call x1, Pallas kernels, body(): pl.pallas_call(write_out, out_shape=(jax.ShapeDtypeStruct((1, BS, BS), F3...  4.42 us

profile of v3, /device:TPU:1, one launch (start us, length us, event | category | flops | bytes accessed | tf_op | source)
XLA Modules:
  0.0 67.4 jit_solution(13589503113397492600)
XLA Ops:
  0.6 0.0 copy-start
  0.6 62.3 %shampoo_step.1 = (f32[1,1024,1024]{2,1,0:T(8,128)S(1)}, f32[1,1024,1024]{2,1,0:T(8,128)S(1)}, bf16[128,8,1024]{2,1,0:T(8,128)(2,1)S(1)}) custom-call(s32[1,128]{1,0:T(1,128)} %bitcast.1, bf16[1,128,16,1024]{3,2,1,0:T(8,128)(2,1)} %grad_hbm.1, f32[1,1024,1024]{2,1,0:T(8,128)} %lstat_hbm.1, f32[1,1024,1024]{2,1,0:T(8,128)} %rstat_hbm.1, ...), custom_call_target="tpu_custom_call" | custom-call | flops 8589934592 | bytes 16777216 | tf_op jit(solution)/shard_map/shampoo_step/pallas_call | solution.py:211
  63.0 0.0 copy-done
  63.0 4.4 %write_out.1 = (f32[1,1024,1024]{2,1,0:T(8,128)}, f32[1,1024,1024]{2,1,0:T(8,128)}, bf16[128,8,1024]{2,1,0:T(8,128)(2,1)}) custom-call(s32[128]{0:T(128)S(1)} %copy-done, f32[1,1024,1024]{2,1,0:T(8,128)S(1)} %get-tuple-element.6.left, f32[1,1024,1024]{2,1,0:T(8,128)S(1)} %get-tuple-element.7.right, bf16[128,8,1024]{2,1,0:T(8,128)(2,1)S(1)} %get-tuple-element.8.returned), custom_call_target="tpu_custom_call" | custom-call | tf_op jit(solution)/shard_map/write_out/pallas_call | solution.py:249
Async XLA Ops:
  0.6 62.3 %copy-start = (s32[128]{0:T(128)S(1)}, s32[128]{0:T(128)}, u32[]{:S(2)}) copy-start(s32[128]{0:T(128)} %owner_of.1) | copy-start | bytes 1540

commit v4 on v2

--- a/solution.py
+++ b/solution.py
@@ -12,7 +12,8 @@
 ROWS = BS // CHIPS
 HALF = ROWS // 2
 CHUNK = 8
-LEAP = 27
+LGR_CHUNK = 16
+LEAP = 53
 BF16 = jnp.bfloat16
 F32 = jnp.float32
 
@@ -25,11 +26,19 @@
     return z * 16 + x * 4 + y
 
 
+def source_chip(me, step):
+    o = lax.rem(step * LEAP, CHIPS)
+    z = lax.rem(lax.div(me, 16) + 4 - lax.div(o, 16), 4)
+    x = lax.rem(lax.div(me, 4) + 8 - lax.rem(lax.div(o, 4), 4), 4)
+    y = lax.rem(me + 4 - lax.rem(o, 4), 4)
+    return z * 16 + x * 4 + y
+
+
 def kernel(
-    owner_of, grad_hbm, lstat_hbm, rstat_hbm, lroot_hbm, rroot_hbm,
+    owner_hbm, grad_hbm, lstat_hbm, rstat_hbm, lroot_hbm, rroot_hbm,
     new_left, new_right, returned,
     grad, stage, partner_part, summed, gathered, lroot, lperm, rroot, outgoing,
-    by_owner_v, by_owner,
+    owner_of, by_owner_v, by_owner,
     load_sem, swap_send, swap_recv, fwd_send, fwd_recv, back_send, back_recv,
 ):
     f = lax.axis_index("fsdp")
@@ -37,16 +46,19 @@
     other = 1 - r
     me = 2 * f + r
 
+    load_owner = pltpu.make_async_copy(owner_hbm, owner_of, load_sem.at[6])
+    load_owner.start()
     load_grad = pltpu.make_async_copy(grad_hbm.at[0], grad, load_sem.at[0])
     load_grad.start()
 
     barrier = pltpu.get_barrier_semaphore()
 
-    @pl.loop(1, 2 * CHIPS)
+    pl.semaphore_signal(barrier, inc=1, device_id=(f, other), device_id_type=MESH)
+
+    @pl.loop(1, CHIPS)
     def _(k):
-        d = lax.rem(me + k, 2 * CHIPS)
         pl.semaphore_signal(
-            barrier, inc=1, device_id=(lax.div(d, 2), lax.rem(d, 2)), device_id_type=MESH
+            barrier, inc=1, device_id=(source_chip(f, k), lax.rem(k, 2)), device_id_type=MESH
         )
 
     loads = [
@@ -55,8 +67,7 @@
         pltpu.make_async_copy(lstat_hbm.at[0], new_left.at[0], load_sem.at[3]),
         pltpu.make_async_copy(rstat_hbm.at[0], new_right.at[0], load_sem.at[4]),
     ]
-    for load in loads:
-        load.start()
+    load_owner.wait()
     slot = lax.broadcasted_iota(jnp.int32, (BLOCKS, BLOCKS), 0)
     block = lax.broadcasted_iota(jnp.int32, (BLOCKS, BLOCKS), 1)
     held = jnp.where(jnp.broadcast_to(owner_of[...], (BLOCKS, BLOCKS)) == slot, block, 0)
@@ -65,7 +76,16 @@
     to_smem.start()
     to_smem.wait()
     load_grad.wait()
-    pl.semaphore_wait(barrier, 2 * CHIPS - 1)
+    for load in loads:
+        load.start()
+
+    @pl.when(r == 0)
+    def _():
+        pl.semaphore_wait(barrier, CHIPS - 1)
+
+    @pl.when(r == 1)
+    def _():
+        pl.semaphore_wait(barrier, CHIPS + 1)
 
     def swap(c):
         part = pl.ds(c * CHUNK, CHUNK)
@@ -74,12 +94,16 @@
             device_id=(f, other), device_id_type=MESH,
         )
 
+    def target(p, core):
+        return partner_chip(f, 2 * lax.rem(p, CHIPS // 2) + core), lax.div(p, CHIPS // 2)
+
     @pl.loop(0, CHIPS // CHUNK)
     def _(c):
         @pl.loop(0, CHUNK)
         def _(j):
-            i = c * CHUNK + j
-            stage[i] = grad[by_owner[0, 2 * partner_chip(f, i) + other]]
+            p = c * CHUNK + j
+            to, core = target(p, other)
+            stage[p] = grad[by_owner[0, 2 * to + core]]
 
         swap(c).start()
 
@@ -89,19 +113,22 @@
 
         @pl.loop(0, CHUNK)
         def _(j):
-            i = c * CHUNK + j
-            to = partner_chip(f, i)
-            mine = grad[by_owner[0, 2 * to + r]].astype(F32)
-            summed[i] = (mine + partner_part[i].astype(F32)).astype(BF16)
-
-            @pl.when(i > 0)
+            p = c * CHUNK + j
+            to, core = target(p, r)
+            mine = grad[by_owner[0, 2 * to + core]].astype(F32)
+            summed[p] = (mine + partner_part[p].astype(F32)).astype(BF16)
+
+            @pl.when(p + r > 0)
             def _():
                 pltpu.make_async_remote_copy(
-                    summed.at[i], gathered.at[f], fwd_send, fwd_recv,
-                    device_id=(to, r), device_id_type=MESH,
+                    summed.at[p], gathered.at[f], fwd_send.at[core], fwd_recv,
+                    device_id=(to, core), device_id_type=MESH,
                 ).start()
 
-    gathered[f] = summed[0]
+    @pl.when(r == 0)
+    def _():
+        gathered[f] = summed[0]
+
     for load in loads:
         load.wait()
 
@@ -110,19 +137,26 @@
         lperm[i] = lroot[pl.ds(pl.multiple_of(partner_chip(f, i) * ROWS, ROWS), ROWS), :]
 
     rest = pl.ds(0, CHIPS - 1)
-    pltpu.make_async_copy(gathered.at[rest], gathered.at[rest], fwd_recv).wait()
-
-    @pl.loop(0, CHIPS // CHUNK)
-    def _(c):
-        part = lperm[pl.ds(c * CHUNK, CHUNK)].reshape(CHUNK * ROWS, BS)
+
+    @pl.when(r == 0)
+    def _():
+        pltpu.make_async_copy(gathered.at[rest], gathered.at[rest], fwd_recv).wait()
+
+    @pl.when(r == 1)
+    def _():
+        pltpu.make_async_copy(gathered, gathered, fwd_recv).wait()
+
+    @pl.loop(0, CHIPS // LGR_CHUNK)
+    def _(c):
+        part = lperm[pl.ds(c * LGR_CHUNK, LGR_CHUNK)].reshape(LGR_CHUNK * ROWS, BS)
         whole = gathered[...].reshape(BS, BS)
         applied = jnp.dot(part, whole, preferred_element_type=F32).astype(BF16)
         done = jnp.dot(applied, rroot[...], preferred_element_type=F32)
-        outgoing[pl.ds(c * 2 * CHUNK, 2 * CHUNK)] = done.reshape(2 * CHUNK, HALF, BS).astype(BF16)
-
-        @pl.loop(0, 2 * CHUNK)
+        outgoing[pl.ds(c * 2 * LGR_CHUNK, 2 * LGR_CHUNK)] = done.reshape(2 * LGR_CHUNK, HALF, BS).astype(BF16)
+
+        @pl.loop(0, 2 * LGR_CHUNK)
         def _(j):
-            h = c * 2 * CHUNK + j
+            h = c * 2 * LGR_CHUNK + j
             to = partner_chip(f, lax.div(h, 2))
             core = lax.rem(h, 2)
 
@@ -155,7 +189,18 @@
     def _(c):
         swap(c).wait_send()
 
-    pltpu.make_async_copy(gathered.at[rest], gathered.at[rest], fwd_send).wait()
+    half = pl.ds(0, CHIPS // 2)
+    half_less = pl.ds(0, CHIPS // 2 - 1)
+
+    @pl.when(r == 0)
+    def _():
+        pltpu.make_async_copy(summed.at[half_less], summed.at[half_less], fwd_send.at[0]).wait()
+
+    @pl.when(r == 1)
+    def _():
+        pltpu.make_async_copy(summed.at[half], summed.at[half], fwd_send.at[0]).wait()
+
+    pltpu.make_async_copy(summed.at[half], summed.at[half], fwd_send.at[1]).wait()
     all_but_me = pl.ds(0, BLOCKS - 1)
     pltpu.make_async_copy(returned.at[all_but_me], returned.at[all_but_me], back_send).wait()
     pltpu.make_async_copy(returned.at[all_but_me], returned.at[all_but_me], back_recv).wait()
@@ -189,7 +234,7 @@
             pltpu.VMEM((1, BS, BS), F32),
             pltpu.VMEM((BLOCKS, HALF, BS), BF16),
         ),
-        in_specs=[vmem] + [anywhere] * 5,
+        in_specs=[anywhere] * 6,
         out_specs=(vmem, vmem, vmem),
         scratch_shapes=[
             pltpu.VMEM((BLOCKS, ROWS, BS), BF16),
@@ -202,11 +247,12 @@
             pltpu.VMEM((BS, BS), BF16),
             pltpu.VMEM((BLOCKS, HALF, BS), BF16),
             pltpu.VMEM((1, BLOCKS), jnp.int32),
+            pltpu.VMEM((1, BLOCKS), jnp.int32),
             pltpu.SMEM((1, BLOCKS), jnp.int32),
-            pltpu.SemaphoreType.DMA((6,)),
+            pltpu.SemaphoreType.DMA((7,)),
             pltpu.SemaphoreType.DMA((CHIPS // CHUNK,)),
             pltpu.SemaphoreType.DMA((CHIPS // CHUNK,)),
-            pltpu.SemaphoreType.DMA,
+            pltpu.SemaphoreType.DMA((2,)),
             pltpu.SemaphoreType.DMA,
             pltpu.SemaphoreType.DMA,
             pltpu.SemaphoreType.DMA,

time: 72.6 us -> 67.1 us (0.924)
  Pallas kernels: 71.8 us -> 66.4 us
    pallas_call x1, Pallas kernels: 67.4 us -> 61.9 us  [body(): pl.pallas_call(kernel, out_shape=(pltpu.VMEM((1, BS, BS), F32), pltpu.VME...]
where the time goes in v4:
time: 67.1 us; the launch traced here: 67 us
  Pallas kernels  66.4 us (99%)
    pallas_call x1, Pallas kernels, body(): pl.pallas_call(kernel, out_shape=(pltpu.VMEM((1, BS, BS), F32), pltpu.VME...  61.9 us
    pallas_call x1, Pallas kernels, body(): pl.pallas_call(write_out, out_shape=(jax.ShapeDtypeStruct((1, BS, BS), F3...  4.42 us

profile of v4, /device:TPU:1, one launch (start us, length us, event | category | flops | bytes accessed | tf_op | source)
XLA Modules:
  0.0 67.0 jit_solution(12725753511134765512)
XLA Ops:
  0.6 0.0 copy-start
  0.6 61.9 %shampoo_step.1 = (f32[1,1024,1024]{2,1,0:T(8,128)S(1)}, f32[1,1024,1024]{2,1,0:T(8,128)S(1)}, bf16[128,8,1024]{2,1,0:T(8,128)(2,1)S(1)}) custom-call(s32[1,128]{1,0:T(1,128)} %bitcast.1, bf16[1,128,16,1024]{3,2,1,0:T(8,128)(2,1)} %grad_hbm.1, f32[1,1024,1024]{2,1,0:T(8,128)} %lstat_hbm.1, f32[1,1024,1024]{2,1,0:T(8,128)} %rstat_hbm.1, ...), custom_call_target="tpu_custom_call" | custom-call | flops 8589934592 | bytes 16777216 | tf_op jit(solution)/shard_map/shampoo_step/pallas_call | solution.py:230
  62.6 0.0 copy-done
  62.6 4.4 %write_out.1 = (f32[1,1024,1024]{2,1,0:T(8,128)}, f32[1,1024,1024]{2,1,0:T(8,128)}, bf16[128,8,1024]{2,1,0:T(8,128)(2,1)}) custom-call(s32[128]{0:T(128)S(1)} %copy-done, f32[1,1024,1024]{2,1,0:T(8,128)S(1)} %get-tuple-element.6.left, f32[1,1024,1024]{2,1,0:T(8,128)S(1)} %get-tuple-element.7.right, bf16[128,8,1024]{2,1,0:T(8,128)(2,1)S(1)} %get-tuple-element.8.returned), custom_call_target="tpu_custom_call" | custom-call | tf_op jit(solution)/shard_map/write_out/pallas_call | solution.py:268
Async XLA Ops:
  0.6 62.0 %copy-start = (s32[128]{0:T(128)S(1)}, s32[128]{0:T(128)}, u32[]{:S(2)}) copy-start(s32[128]{0:T(128)} %owner_of.1) | copy-start | bytes 1540
